TPU v7x, 32 devices: a whole 2x2x4 slice. The times are simulated.
32 devices in a mesh: attn: 4 (over z), expert: 8 (over y, x, core).
Axes of the slice: x: 2, y: 2, z: 4, core: 2. Of those that a mesh axis runs over, the one named last changes fastest.
Arguments:
- tokens: bfloat16 [8, 512, 2048], P('expert', 'attn'), may hold values from -3 to 5
- lengths: int32 [8, 3], P('expert'), may hold values from 1 to 384, 512 in all within a row
- page_table: int32 [8, 3, 4], P('expert'), may hold values from 0 to 11, as said below
- routes: int32 [8, 512, 6], P('expert'), may hold values from 0 to 63, all different within a row; in each aligned block of 512 rows (0 to 511, 512 to 1023, ..., all dimensions but the last counted through in order) at most 56 rows name the same one
- attn_gain: bfloat16 [2048], replicated, may hold values from 0.099609375 to 1.8984375
- w_query: bfloat16 [2048, 3072], P(None, 'attn'), may hold values from -0.125 to 0.125
- w_latent: bfloat16 [2048, 576], replicated, may hold values from -0.125 to 0.125
- latent_gain: bfloat16 [512], replicated, may hold values from 0.099609375 to 1.8984375
- w_key: bfloat16 [512, 2048], P(None, 'attn'), may hold values from -0.25 to 0.25
- w_value: bfloat16 [512, 2048], P(None, 'attn'), may hold values from -0.25 to 0.25
- w_out: bfloat16 [2048, 2048], P('attn'), may hold values from -0.125 to 0.125
- ffn_gain: bfloat16 [2048], replicated, may hold values from 0.099609375 to 1.8984375
- w_router: bfloat16 [2048, 64], replicated, may hold values from -0.08985319 to 0.08985319
- expert_gate: bfloat16 [64, 2048, 1408], P('expert', None, 'attn'), may hold values from -0.375 to 0.375
- expert_up: bfloat16 [64, 2048, 1408], P('expert', None, 'attn'), may hold values from -0.375 to 0.375
- expert_down: bfloat16 [64, 1408, 2048], P('expert', 'attn'), may hold values from -7.462025 to 7.462025
- shared_gate: bfloat16 [2048, 1408], P(None, 'attn'), may hold values from -0.125 to 0.125
- shared_up: bfloat16 [2048, 1408], P(None, 'attn'), may hold values from -0.125 to 0.125
- shared_down: bfloat16 [1408, 2048], P('attn'), may hold values from -0.15625 to 0.15625
Outputs:
- layer_out: bfloat16 [8, 512, 2048], P('expert', 'attn')
- latent_pages: bfloat16 [8, 12, 128, 512], P('expert', 'attn')
- rope_pages: bfloat16 [8, 12, 64, 128], P('expert', 'attn')
Inputs may be any that keep to these rules, and one draw needn't show every extreme that they name: `page_table`: each group's table holds every slot 0 to 11 exactly once; entries past a prompt's last page are unused. The 3 lengths of a group sum to 512 and the longest is exactly 384. `routes`: a row names 6 different experts; within one group's 512 rows no expert is named more than 56 times, a bound that some block reaches.
All inputs are finite; a program needn't handle non-finite values.
Results may differ from a plain program's by a relative error of at most 0.029.
Values may be sent and summed in bfloat16 or wider, within the bound.
A program may use at most 192 MiB of HBM per device.

v0:
```python
import math

import jax
import jax.numpy as jnp
from jax import lax
from jax.sharding import PartitionSpec as P

NOPE = 128
ROPE = 64
VDIM = 128
LAT = 512
EXPERTS = 64
TOP = 6
PAGE = 128


epsilon = 1e-06


def rms_apply(values, gain_vec):
    mean_square = jnp.mean(values * values, axis=-1, keepdims=True)
    return values * lax.rsqrt(mean_square + epsilon) * gain_vec.astype(jnp.float32)


def rope_tables(positions, width_rope):
    half_width = width_rope // 2
    freq_index = jnp.arange(half_width, dtype=jnp.float32)
    inverse_freq = jnp.exp(freq_index * (-2.0 * math.log(10000.0) / width_rope))
    angles = positions.astype(jnp.float32)[:, None] * inverse_freq[None, :]
    return (jnp.cos(angles), jnp.sin(angles))


def rope_apply(values, cosine, sine):
    half_width = values.shape[-1] // 2
    first_half = values[..., :half_width]
    second_half = values[..., half_width:]
    return jnp.concatenate(
        [first_half * cosine - second_half * sine, second_half * cosine + first_half * sine],
        axis=-1,
    )


def write_pages(latent, key_rope, seg_lengths, starts, table, slot_ids, page_len):
    seg_count = table.shape[0]
    pages_per = table.shape[1]
    match = table[None, :, :] == slot_ids[:, None, None]
    seg_pick = jnp.sum(
        jnp.where(match, jnp.arange(seg_count, dtype=jnp.int32)[None, :, None], 0), axis=(1, 2)
    )
    page_pick = jnp.sum(
        jnp.where(match, jnp.arange(pages_per, dtype=jnp.int32)[None, None, :], 0), axis=(1, 2)
    )
    seg_match = seg_pick[:, None] == jnp.arange(seg_count, dtype=jnp.int32)[None, :]
    first_row = jnp.sum(jnp.where(seg_match, starts[None, :], 0), axis=1)
    seg_len = jnp.sum(jnp.where(seg_match, seg_lengths[None, :], 0), axis=1)
    offsets = page_pick[:, None] * page_len + jnp.arange(page_len, dtype=jnp.int32)[None, :]
    valid = offsets < seg_len[:, None]
    row_index = jnp.minimum(first_row[:, None] + offsets, latent.shape[0] - 1)
    latent_rows = jnp.take(latent, row_index, axis=0)
    rope_rows = jnp.take(key_rope, row_index, axis=0)
    zero_value = jnp.zeros((), latent.dtype)
    latent_out = jnp.where(valid[:, :, None], latent_rows, zero_value)
    rope_out = jnp.where(valid[:, None, :], jnp.transpose(rope_rows, (0, 2, 1)), zero_value)
    return (latent_out, rope_out)


def local(
    tokens,
    lengths,
    page_table,
    routes,
    attn_gain,
    w_query,
    w_latent,
    latent_gain,
    w_key,
    w_value,
    w_out,
    ffn_gain,
    w_router,
    expert_gate,
    expert_up,
    expert_down,
    shared_gate,
    shared_up,
    shared_down,
):
    quarters = lax.axis_size("attn")
    rank_attn = lax.axis_index("attn")
    owners = lax.axis_size("expert")
    own_rows = tokens.shape[1]
    group_rows = own_rows * quarters
    heads_here = w_value.shape[1] // VDIM
    local_experts = expert_gate.shape[0]
    capacity = quarters * (
        (7 * group_rows * TOP + 6 * EXPERTS * quarters - 1) // (6 * EXPERTS * quarters)
    )
    score_scale = (NOPE + ROPE) ** (-0.5)
    first_own = rank_attn * own_rows
    residual_own = tokens[0].astype(jnp.float32)
    normed_own = rms_apply(residual_own, attn_gain).astype(jnp.bfloat16)
    piece = lax.all_gather(normed_own, "attn", axis=0, tiled=True)
    projected = jnp.concatenate(
        [
            jnp.dot(piece, w_query, preferred_element_type=jnp.float32),
            jnp.dot(piece, w_latent, preferred_element_type=jnp.float32),
        ],
        axis=1,
    )
    seg_lengths = lengths[0]
    ends = jnp.cumsum(seg_lengths)
    starts = ends - seg_lengths
    row_ids = jnp.arange(group_rows, dtype=jnp.int32)
    seg_of_row = jnp.sum((row_ids[:, None] >= ends[None, :]).astype(jnp.int32), axis=1)
    seg_match = seg_of_row[:, None] == jnp.arange(seg_lengths.shape[0], dtype=jnp.int32)[None, :]
    positions = row_ids - jnp.sum(jnp.where(seg_match, starts[None, :], 0), axis=1)
    cosine, sine = rope_tables(positions, ROPE)
    query_width = w_query.shape[1]
    query_raw = projected[:, :query_width].reshape(group_rows, heads_here, NOPE + ROPE)
    query_all = jnp.concatenate(
        [
            query_raw[..., :NOPE],
            rope_apply(query_raw[..., NOPE:], cosine[:, None, :], sine[:, None, :]),
        ],
        axis=-1,
    ).astype(jnp.bfloat16)
    compressed = projected[:, query_width:]
    latent = rms_apply(compressed[:, :LAT], latent_gain).astype(jnp.bfloat16)
    key_rope = rope_apply(compressed[:, LAT:], cosine, sine).astype(jnp.bfloat16)
    key_nope = (
        jnp.dot(latent, w_key, preferred_element_type=jnp.float32)
        .astype(jnp.bfloat16)
        .reshape(group_rows, heads_here, NOPE)
    )
    value_rows = (
        jnp.dot(latent, w_value, preferred_element_type=jnp.float32)
        .astype(jnp.bfloat16)
        .reshape(group_rows, heads_here, VDIM)
    )
    slots_here = page_table.shape[1] * page_table.shape[2] // quarters
    slot_ids = rank_attn * slots_here + jnp.arange(slots_here, dtype=jnp.int32)
    latent_out, rope_out = write_pages(
        latent, key_rope, seg_lengths, starts, page_table[0], slot_ids, PAGE
    )
    query_ids = jnp.arange(group_rows, dtype=jnp.int32)
    score_nope = jnp.einsum(
        "qhd,khd->hqk", query_all[..., :NOPE], key_nope, preferred_element_type=jnp.float32
    )
    score_rope = jnp.einsum(
        "qhd,kd->hqk", query_all[..., NOPE:], key_rope, preferred_element_type=jnp.float32
    )
    scores = (score_nope + score_rope) * score_scale
    allowed = (seg_of_row[:, None] == seg_of_row[None, :]) & (
        row_ids[None, :] <= query_ids[:, None]
    )
    weights = jnp.where(allowed[None, :, :], jnp.exp(scores), 0.0)
    probs = (weights / jnp.sum(weights, axis=-1, keepdims=True)).astype(jnp.bfloat16)
    mixed = (
        jnp.einsum("hqk,khd->qhd", probs, value_rows, preferred_element_type=jnp.float32)
        .astype(jnp.bfloat16)
        .reshape(group_rows, heads_here * VDIM)
    )
    term_all = jnp.dot(mixed, w_out, preferred_element_type=jnp.float32)
    own_term = lax.dynamic_slice_in_dim(term_all, first_own, own_rows, 0) + residual_own
    term_all = lax.dynamic_update_slice_in_dim(term_all, own_term, first_own, 0)
    hidden_all = lax.psum(term_all.astype(jnp.bfloat16), "attn").astype(jnp.float32)
    hidden_own = lax.dynamic_slice_in_dim(hidden_all, first_own, own_rows, 0)
    normed_all = rms_apply(hidden_all, ffn_gain).astype(jnp.bfloat16)
    logits = jnp.dot(normed_all, w_router, preferred_element_type=jnp.float32)
    exp_logits = jnp.exp(logits)
    router = exp_logits / jnp.sum(exp_logits, axis=1, keepdims=True)
    route_rows = routes[0]
    expert_ids = jnp.arange(EXPERTS, dtype=jnp.int32)
    route_hits = route_rows[:, :, None] == expert_ids[None, None, :]
    pair_weight = jnp.sum(jnp.where(route_hits, router[:, None, :], 0.0), axis=2).reshape(-1)
    flat_hits = route_hits.reshape(group_rows * TOP, EXPERTS).astype(jnp.int32)
    slot_of_pair = jnp.sum(jnp.cumsum(flat_hits, axis=0) * flat_hits, axis=1) - 1
    pair_expert = route_rows.reshape(-1)
    target = pair_expert * capacity + slot_of_pair
    pair_rows = jnp.repeat(row_ids, TOP)
    source_row = jnp.full((EXPERTS * capacity,), group_rows, jnp.int32).at[target].set(pair_rows)
    padded_rows = jnp.concatenate(
        [normed_all, jnp.zeros((1, normed_all.shape[1]), jnp.bfloat16)], axis=0
    )
    outgoing = jnp.take(padded_rows, source_row, axis=0).reshape(
        owners, local_experts, capacity, normed_all.shape[1]
    )
    arrived = lax.all_to_all(outgoing, "expert", split_axis=0, concat_axis=0, tiled=True)
    gate_act = jnp.einsum(
        "sech,ehf->secf", arrived, expert_gate, preferred_element_type=jnp.float32
    )
    up_act = jnp.einsum("sech,ehf->secf", arrived, expert_up, preferred_element_type=jnp.float32)
    hidden_act = (jax.nn.silu(gate_act) * up_act).astype(jnp.bfloat16)
    worked = jnp.einsum(
        "secf,efh->sech", hidden_act, expert_down, preferred_element_type=jnp.float32
    ).astype(jnp.bfloat16)
    width = normed_all.shape[1]
    results = lax.all_to_all(worked, "expert", split_axis=0, concat_axis=0, tiled=True)
    returned = results.reshape(EXPERTS * capacity, width)
    pair_out = jnp.take(returned, target, axis=0).astype(jnp.float32) * pair_weight[:, None]
    routed = jnp.sum(pair_out.reshape(group_rows, TOP, width), axis=1)
    shared_hidden = (
        jax.nn.silu(jnp.dot(normed_all, shared_gate, preferred_element_type=jnp.float32))
        * jnp.dot(normed_all, shared_up, preferred_element_type=jnp.float32)
    ).astype(jnp.bfloat16)
    ffn_term = routed + jnp.dot(shared_hidden, shared_down, preferred_element_type=jnp.float32)
    ffn_own = lax.psum_scatter(
        ffn_term.astype(jnp.bfloat16), "attn", scatter_dimension=0, tiled=True
    ).astype(jnp.float32)
    layer_out = (hidden_own + ffn_own).astype(jnp.bfloat16)[None]
    return (layer_out, latent_out[None], rope_out[None])


def solution(mesh):
    placed = (
        P("expert", "attn", None),
        P("expert", None),
        P("expert", None, None),
        P("expert", None, None),
        P(),
        P(None, "attn"),
        P(),
        P(),
        P(None, "attn"),
        P(None, "attn"),
        P("attn", None),
        P(),
        P(),
        P("expert", None, "attn"),
        P("expert", None, "attn"),
        P("expert", "attn", None),
        P(None, "attn"),
        P(None, "attn"),
        P("attn", None),
    )
    return jax.shard_map(
        local,
        mesh=mesh,
        in_specs=placed,
        out_specs=(
            P("expert", "attn", None),
            P("expert", "attn", None, None),
            P("expert", "attn", None, None),
        ),
        check_vma=False,
    )
```

profile of v0, /device:TPU:0, one launch (start us, length us, event | category | flops | bytes accessed | tf_op | source)
XLA Modules:
  0.0 707.9 jit_solution(4364200759180468323)
XLA Ops:
  7.2 0.8 convert_element_type.89
  8.1 1.3 fusion.28
  9.4 2.0 fusion.30
  11.5 0.8 copy.89
  12.3 0.2 eq.97
  12.5 0.2 reshape_squeeze.6
  12.7 0.7 convert_element_type.91
  13.4 0.8 reduce-window.10
  14.2 0.7 convert_element_type.103
  14.9 1.0 fusion.35
  15.8 34.8 %reduce-window.11 = s32[64,24,128]{2,1,0:T(8,128)} reduce-window(s32[64,24,128]{2,1,0:T(8,128)} %fusion.35, s32[]{:T(128)} %constant.55.clone.1), window={size=1x1x128 pad=0_0x0_0x127_0}, to_apply=%region_7.8 | reduce-window | flops 24969216 | bytes 1572868 | tf_op jit(solution)/shard_map/reduce-window.1
  50.7 2.3 slice.56
  53.0 1.6 copy.110
  54.6 0.2 reduce-window.14
  55.0 0.4 copy-done.18
  55.4 0.2 fusion.32
  55.6 4.6 all-gather.2.cloned.1.call-done
  60.2 3.8 fusion.55
  64.3 0.5 convolution_convert_fusion
  64.8 0.3 copy-done.4
  65.1 1.3 convolution_convert_fusion.1
  66.4 0.3 subtract_convert_fusion.1
  66.8 1.8 fusion.56
  68.6 0.8 fusion.37
  69.5 3.3 fusion.13
  72.8 4.4 fusion.26
  77.2 1.3 fusion.57
  78.5 0.2 fusion.31
  78.7 1.7 convert_element_type.100
  80.5 0.2 mul.229
  80.8 0.2 reshape.470
  80.9 0.3 broadcast_add_fusion
  81.4 12.0 %scatter_custom_fusion = s32[3584]{0:T(1024)S(1)} fusion(s32[3072]{0:T(1024)S(1)} %bitcast.142, s32[3072]{0:T(1024)S(1)} %reshape.470, s32[]{:T(128)} %constant.67.clone.1), kind=kCustom, calls=%fused_computation.85 | custom fusion | bytes 14340 | tf_op jit(solution)/shard_map/scatter | solution.py:181
  93.6 72.6 %all-reduce.3.cloned.1.call-done = bf16[512,2048]{1,0:T(8,128)(2,1)} async-done(((bf16[512,2048]{1,0:T(8,128)(2,1)}), bf16[512,2048]{1,0:T(8,128)(2,1)}) %all-reduce.3.cloned.1.call-update) | async-done | bytes 2097168 | tf_op jit(solution)/shard_map/psum | solution.py:166
  166.2 2.1 multiply_reduce_fusion.1
  168.2 2.1 multiply_convert_fusion
  170.4 1.3 copy-done.2
  171.9 14.5 %gather_fusion = bf16[3584,2048]{1,0:T(8,128)(2,1)} fusion(bf16[513,2048]{1,0:T(8,128)(2,1)S(1)} %concatenate.14, s32[4096]{0:T(1024)S(1)} %pad_clamp_fusion), kind=kCustom, calls=%fused_computation | custom fusion | bytes 29374464 | tf_op jit(solution)/shard_map/jit(_take)/gather | solution.py:185
  186.4 7.7 %broadcast_select_fusion = bf16[8,8,56,2048]{3,2,1,0:T(8,128)(2,1)S(1)} fusion(bf16[8,8,56,2048]{3,2,1,0:T(8,128)(2,1)} %bitcast.129, pred[8,8,56]{2,1,0:T(8,128)(4,1)S(1)} %broadcast_in_dim.207), kind=kLoop, calls=%fused_computation.7 | loop fusion | flops 7340032 | bytes 29363712 | tf_op jit(solution)/shard_map/jit(_take)/select_n | solution.py:185
  194.2 165.1 %all_to_all.10 = bf16[8,8,56,2048]{3,2,1,0:T(8,128)(2,1)} all-to-all(bf16[8,8,56,2048]{3,2,1,0:T(8,128)(2,1)S(1)} %broadcast_select_fusion), channel_id=1, replica_groups=mesh['attn'=4,'expert'=8] {'expert'}, dimensions={0} | all-to-all | bytes 29360128 | tf_op jit(solution)/shard_map/all_to_all | solution.py:188
  359.3 14.2 %fusion = f32[8,8,56,352]{3,2,1,0:T(8,128)} fusion(bf16[8,8,56,2048]{3,2,1,0:T(8,128)(2,1)} %all_to_all.10, bf16[8,2048,352]{1,2,0:T(8,128)(2,1)} %param.33), kind=kOutput, calls=%fused_computation.8 | convolution fusion | flops 5167382528 | bytes 31260672 | tf_op jit(solution)/shard_map/sech,ehf->secf/dot_general | solution.py:192
  373.4 24.7 %convert_bitcast_fusion = bf16[8,8,56,2048]{3,2,0,1:T(8,128)(2,1)} fusion(bf16[8,352,2048]{2,1,0:T(8,128)(2,1)} %param.34, f32[8,8,56,352]{3,2,1,0:T(8,128)} %fusion, bf16[8,8,56,2048]{3,2,1,0:T(8,128)(2,1)} %all_to_all.10, bf16[8,2048,352]{1,2,0:T(8,128)(2,1)} %param.32), kind=kOutput, calls=%fused_computation.6 | convolution fusion | flops 10349674496 | bytes 57475072 | tf_op jit(solution)/shard_map/secf,efh->sech/dot_general | solution.py:194
  398.1 13.5 %copy.98 = bf16[8,8,56,2048]{3,2,1,0:T(8,128)(2,1)} copy(bf16[8,8,56,2048]{3,2,0,1:T(8,128)(2,1)} %convert_bitcast_fusion) | data formatting | bytes 29360128 | tf_op jit(solution)/shard_map/convert_element_type | solution.py:196
  411.6 5.7 all-to-all-start.1
  417.3 0.3 reduce-scatter.2.cloned.1.call-start
  417.5 0.2 sub.30
  417.9 0.2 copy.94
  418.1 0.8 fusion.54
  419.2 3.2 fusion.58
  422.4 156.3 %all-to-all-done.1 = bf16[8,8,56,2048]{3,2,1,0:T(8,128)(2,1)} async-done(((bf16[8,8,56,2048]{3,2,1,0:T(8,128)(2,1)}), bf16[8,8,56,2048]{3,2,1,0:T(8,128)(2,1)}, u32[]{:S(2)}, u32[]{:S(2)}) %all-to-all-start.1) | async-done | bytes 14680096 | tf_op jit(solution)/shard_map/all_to_all | solution.py:198
  578.7 30.9 %gather_fusion.1 = bf16[3072,2048]{1,0:T(8,128)(2,1)} fusion(bf16[3584,2048]{1,0:T(8,128)(2,1)} %bitcast.28, s32[3072]{0:T(1024)S(1)} %broadcast_clamp_fusion), kind=kCustom, calls=%fused_computation.1 | custom fusion | bytes 25178112 | tf_op jit(solution)/shard_map/jit(_take)/gather | solution.py:200
  609.6 20.4 %gather.25 = bf16[512,6,2048]{2,1,0:T(8,128)(2,1)} reshape(bf16[3072,2048]{1,0:T(8,128)(2,1)} %gather_fusion.1) | data formatting | bytes 25165824 | tf_op jit(solution)/shard_map/jit(_take)/gather | solution.py:200
  630.0 21.0 %multiply_reduce_fusion = f32[512,2048]{1,0:T(8,128)} fusion(f32[512,6]{1,0:T(8,128)S(1)} %copy.99, bf16[512,6,2048]{2,1,0:T(8,128)(2,1)} %gather.25, pred[512,6]{1,0:T(8,128)(4,1)S(1)} %copy.94), kind=kLoop, calls=%fused_computation.5 | loop fusion | flops 24117248 | bytes 16792576 | tf_op jit(solution)/shard_map/reduce_sum | solution.py:201
  651.0 6.9 add_convert_fusion
  657.9 0.3 fusion.46
  658.2 0.2 select_reduce_fusion.3
  658.6 0.2 copy.100
  658.9 1.4 gather_fusion.3
  660.5 2.1 gather_fusion.2
  662.6 0.6 select_bitcast_fusion
  663.2 0.9 select_select_fusion
  664.1 4.2 convert_element_type.101
  668.3 30.8 %reduce-scatter.2.cloned.1.call-done = bf16[128,2048]{1,0:T(8,128)(2,1)} async-done(((bf16[512,2048]{1,0:T(8,128)(2,1)}), bf16[128,2048]{1,0:T(8,128)(2,1)}) %reduce-scatter.2.cloned.1.call-update) | async-done | bytes 524304 | tf_op jit(solution)/shard_map/reduce_scatter | solution.py:207
  699.1 2.3 fusion.36
  (88 shorter events, 2.3 us)
Async XLA Ops:
  7.2 59.6 %copy-start = (bf16[2048,768]{1,0:T(8,128)(2,1)S(1)}, bf16[2048,768]{1,0:T(8,128)(2,1)}, u32[]{:S(2)}) copy-start(bf16[2048,768]{1,0:T(8,128)(2,1)} %param.24) | copy-start | bytes 9437188
  7.2 47.7 %copy-start.21 = (s32[1,3]{1,0:T(1,128)S(1)}, s32[1,3]{1,0:T(1,128)}, u32[]{:S(2)}) copy-start(s32[1,3]{1,0:T(1,128)} %param.20) | copy-start | bytes 40
  7.2 53.0 %all-gather.2.cloned.1.call-start = ((), (), s32[]{:S(2)}) async-start(), calls=%async_computation.3 | async-start | bytes 2621440 | tf_op jit(solution)/shard_map/all_gather | solution.py:102
  11.4 154.7 %all-reduce.3.cloned.1.call-start = ((), (), s32[]{:S(2)}) async-start(), calls=%async_computation.4 | async-start | bytes 4194304 | tf_op jit(solution)/shard_map/psum | solution.py:166
  54.9 0.5 copy-start.18
  60.2 4.1 copy-start.9
  64.0 1.1 copy-start.10
  64.0 2.7 copy-start.23
  64.3 0.8 copy-start.4
  66.8 2.7 copy-start.12
  66.8 2.7 copy-start.14
  69.5 3.3 copy-start.11
  72.8 4.4 copy-start.8
  77.2 1.3 copy-start.7
  78.7 1.7 copy-start.17
  78.7 2.3 copy-start.6
  170.4 1.4 copy-start.2
  411.6 6.5 copy-start.3
  411.6 6.5 copy-start.16
  411.6 167.2 %all-to-all-start.1 = ((bf16[8,8,56,2048]{3,2,1,0:T(8,128)(2,1)}), bf16[8,8,56,2048]{3,2,1,0:T(8,128)(2,1)}, u32[]{:S(2)}, u32[]{:S(2)}) async-start(bf16[8,8,56,2048]{3,2,1,0:T(8,128)(2,1)} %copy.98), calls=%async_computation.1 | async-start | bytes 29360128 | tf_op jit(solution)/shard_map/all_to_all | solution.py:198
  417.3 281.8 %reduce-scatter.2.cloned.1.call-start = ((), (), s32[]{:S(2)}) async-start(), calls=%async_computation.5 | async-start | bytes 2621440 | tf_op jit(solution)/shard_map/reduce_scatter | solution.py:207
  651.0 6.9 copy-start.20
  651.0 7.2 %copy-start.19 = (s32[3]{0:T(128)S(1)}, s32[3]{0:T(128)}, u32[]{:S(2)}) copy-start(s32[3]{0:T(128)} %copy-done.18) | copy-start | bytes 40
  651.0 7.2 %copy-start.22 = (s32[1,3]{1,0:T(1,128)S(1)}, s32[1,3]{1,0:T(1,128)}, u32[]{:S(2)}) copy-start(s32[1,3]{1,0:T(1,128)} %param.20) | copy-start | bytes 40
  651.0 7.6 %copy-start.5 = (bf16[512,512]{0,1:T(8,128)(2,1)S(1)}, bf16[512,512]{0,1:T(8,128)(2,1)}, u32[]{:S(2)}) copy-start(bf16[512,512]{0,1:T(8,128)(2,1)} %copy-done.4) | copy-start | bytes 1572868
  651.0 7.8 %copy-start.13 = (bf16[512,32]{0,1:T(8,128)(2,1)S(1)}, bf16[512,32]{0,1:T(8,128)(2,1)}, u32[]{:S(2)}) copy-start(bf16[512,32]{0,1:T(8,128)(2,1)} %copy-done.12) | copy-start | bytes 98308
  651.0 7.8 %copy-start.15 = (bf16[512,32]{0,1:T(8,128)(2,1)S(1)}, bf16[512,32]{0,1:T(8,128)(2,1)}, u32[]{:S(2)}) copy-start(bf16[512,32]{0,1:T(8,128)(2,1)} %copy-done.14) | copy-start | bytes 98308
  663.2 38.2 %copy-start.1 = (bf16[2048,768]{1,0:T(8,128)(2,1)S(1)}, bf16[2048,768]{1,0:T(8,128)(2,1)}, u32[]{:S(2)}) copy-start(bf16[2048,768]{1,0:T(8,128)(2,1)} %param.24) | copy-start | bytes 9437188
Sparse Core Ops, SparseCore 0:
  11.6 48.6 all-gather.1
  80.5 85.6 all-reduce.2
  658.0 41.0 reduce-scatter.1
where the time goes:
time: 712 us; the launch traced here: 708 us
  waiting for transfers between devices  264 us (37%)
  blocking collectives  165 us (23%)
  local copies, waits for them, and re-layouts  104 us (15%)
  other arithmetic  87.5 us (12%)
  matrix products  66.7 us (9%)
  between operations  14.4 us (2%)
    all_to_all x1, blocking collectives, local(): lax.all_to_all(outgoing, 'expert', split_axis=0, concat_axis=0, tiled=True)  165 us
    all_to_all x1, waiting for transfers between devices, local(): lax.all_to_all(worked, 'expert', split_axis=0, concat_axis=0, tiled=True)  156 us
    psum x1, waiting for transfers between devices, local(): lax.psum(term_all.astype(jnp.bfloat16), 'attn').astype(jnp.float32)  72.6 us
    gather x2, local copies, waits for them, and re-layouts, local(): jnp.take(returned, target, axis=0).astype(jnp.float32)  51.2 us
    another operation x6, other arithmetic  36.5 us
    reduce_scatter x1, waiting for transfers between devices, local(): lax.psum_scatter(ffn_term.astype(jnp.bfloat16), 'attn', scatter_dimension...  30.8 us
    dot_general x1, matrix products, local(): jnp.einsum('secf,efh->sech', hidden_act, expert_down, preferred_element_t...  24.7 us
    reduce_sum x1, other arithmetic, local(): routed = jnp.sum(pair_out.reshape(group_rows, TOP, width), axis=1)  21 us
  transfers between devices with their start and end apart: 4, of which 4 were waited for; matrix products, arithmetic and copies ran while one was open for 10% of the time, Pallas kernels for 0%

commit v1 on v0

--- a/solution.py
+++ b/solution.py
@@ -62,6 +62,19 @@
     latent_out = jnp.where(valid[:, :, None], latent_rows, zero_value)
     rope_out = jnp.where(valid[:, None, :], jnp.transpose(rope_rows, (0, 2, 1)), zero_value)
     return (latent_out, rope_out)
+
+
+def pick_matrix(routes_all, first_expert, local_experts, capacity):
+    ids = first_expert + jnp.arange(local_experts, dtype=jnp.int32)
+    hits = jnp.any(routes_all[:, None, :, :] == ids[None, :, None, None], axis=3)
+    row_ids = jnp.arange(hits.shape[2], dtype=jnp.int32)
+    earlier = (row_ids[:, None] < row_ids[None, :]).astype(jnp.bfloat16)
+    before = jnp.einsum(
+        "gek,kr->ger", hits.astype(jnp.bfloat16), earlier, preferred_element_type=jnp.float32
+    ).astype(jnp.int32)
+    slots = jnp.where(hits, before, -1)
+    wanted = jnp.arange(capacity, dtype=jnp.int32)
+    return (slots[:, :, None, :] == wanted[None, None, :, None]).astype(jnp.bfloat16)
 
 
 def local(
@@ -96,7 +109,8 @@
         (7 * group_rows * TOP + 6 * EXPERTS * quarters - 1) // (6 * EXPERTS * quarters)
     )
     score_scale = (NOPE + ROPE) ** (-0.5)
-    first_own = rank_attn * own_rows
+    routes_all = lax.all_gather(routes[0], "expert", axis=0)
+    first_expert = lax.axis_index("expert") * local_experts
     residual_own = tokens[0].astype(jnp.float32)
     normed_own = rms_apply(residual_own, attn_gain).astype(jnp.bfloat16)
     piece = lax.all_gather(normed_own, "attn", axis=0, tiled=True)
@@ -108,7 +122,10 @@
         axis=1,
     )
     seg_lengths = lengths[0]
-    ends = jnp.cumsum(seg_lengths)
+    seg_ids = jnp.arange(seg_lengths.shape[0], dtype=jnp.int32)
+    ends = jnp.sum(
+        jnp.where(seg_ids[None, :] <= seg_ids[:, None], seg_lengths[None, :], 0), axis=1
+    )
     starts = ends - seg_lengths
     row_ids = jnp.arange(group_rows, dtype=jnp.int32)
     seg_of_row = jnp.sum((row_ids[:, None] >= ends[None, :]).astype(jnp.int32), axis=1)
@@ -161,53 +178,50 @@
         .reshape(group_rows, heads_here * VDIM)
     )
     term_all = jnp.dot(mixed, w_out, preferred_element_type=jnp.float32)
-    own_term = lax.dynamic_slice_in_dim(term_all, first_own, own_rows, 0) + residual_own
-    term_all = lax.dynamic_update_slice_in_dim(term_all, own_term, first_own, 0)
-    hidden_all = lax.psum(term_all.astype(jnp.bfloat16), "attn").astype(jnp.float32)
-    hidden_own = lax.dynamic_slice_in_dim(hidden_all, first_own, own_rows, 0)
-    normed_all = rms_apply(hidden_all, ffn_gain).astype(jnp.bfloat16)
-    logits = jnp.dot(normed_all, w_router, preferred_element_type=jnp.float32)
+    attn_own = lax.psum_scatter(
+        term_all.astype(jnp.bfloat16), "attn", scatter_dimension=0, tiled=True
+    ).astype(jnp.float32)
+    hidden_own = residual_own + attn_own
+    normed_ffn = rms_apply(hidden_own, ffn_gain).astype(jnp.bfloat16)
+    normed_all = lax.all_gather(normed_ffn, "attn", axis=0, tiled=True)
+    rows_all = lax.all_gather(normed_all, "expert", axis=0)
+    width = normed_all.shape[1]
+
+    picks = pick_matrix(routes_all, first_expert, local_experts, capacity)
+
+    logits = jnp.einsum("grd,dx->grx", rows_all, w_router, preferred_element_type=jnp.float32)
     exp_logits = jnp.exp(logits)
-    router = exp_logits / jnp.sum(exp_logits, axis=1, keepdims=True)
-    route_rows = routes[0]
-    expert_ids = jnp.arange(EXPERTS, dtype=jnp.int32)
-    route_hits = route_rows[:, :, None] == expert_ids[None, None, :]
-    pair_weight = jnp.sum(jnp.where(route_hits, router[:, None, :], 0.0), axis=2).reshape(-1)
-    flat_hits = route_hits.reshape(group_rows * TOP, EXPERTS).astype(jnp.int32)
-    slot_of_pair = jnp.sum(jnp.cumsum(flat_hits, axis=0) * flat_hits, axis=1) - 1
-    pair_expert = route_rows.reshape(-1)
-    target = pair_expert * capacity + slot_of_pair
-    pair_rows = jnp.repeat(row_ids, TOP)
-    source_row = jnp.full((EXPERTS * capacity,), group_rows, jnp.int32).at[target].set(pair_rows)
-    padded_rows = jnp.concatenate(
-        [normed_all, jnp.zeros((1, normed_all.shape[1]), jnp.bfloat16)], axis=0
-    )
-    outgoing = jnp.take(padded_rows, source_row, axis=0).reshape(
-        owners, local_experts, capacity, normed_all.shape[1]
-    )
-    arrived = lax.all_to_all(outgoing, "expert", split_axis=0, concat_axis=0, tiled=True)
-    gate_act = jnp.einsum(
-        "sech,ehf->secf", arrived, expert_gate, preferred_element_type=jnp.float32
-    )
-    up_act = jnp.einsum("sech,ehf->secf", arrived, expert_up, preferred_element_type=jnp.float32)
-    hidden_act = (jax.nn.silu(gate_act) * up_act).astype(jnp.bfloat16)
-    worked = jnp.einsum(
-        "secf,efh->sech", hidden_act, expert_down, preferred_element_type=jnp.float32
-    ).astype(jnp.bfloat16)
-    width = normed_all.shape[1]
-    results = lax.all_to_all(worked, "expert", split_axis=0, concat_axis=0, tiled=True)
-    returned = results.reshape(EXPERTS * capacity, width)
-    pair_out = jnp.take(returned, target, axis=0).astype(jnp.float32) * pair_weight[:, None]
-    routed = jnp.sum(pair_out.reshape(group_rows, TOP, width), axis=1)
+    router = exp_logits / jnp.sum(exp_logits, axis=-1, keepdims=True)
+    router_here = lax.dynamic_slice_in_dim(router, first_expert, local_experts, 2)
+    here = jnp.transpose(router_here, (2, 0, 1))
+    slot_weight = jnp.sum(
+        jnp.where(jnp.transpose(picks, (1, 0, 2, 3)) > 0, here[:, :, None, :], 0.0), axis=3
+    ).reshape(local_experts, owners * capacity, 1)
+    arrived = (
+        jnp.einsum("gesr,grd->egsd", picks, rows_all, preferred_element_type=jnp.float32)
+        .astype(jnp.bfloat16)
+        .reshape(local_experts, owners * capacity, width)
+    )
+    gate_act = jnp.einsum("ech,ehf->ecf", arrived, expert_gate, preferred_element_type=jnp.float32)
+    up_act = jnp.einsum("ech,ehf->ecf", arrived, expert_up, preferred_element_type=jnp.float32)
+    hidden_act = (jax.nn.silu(gate_act) * up_act * slot_weight).astype(jnp.bfloat16)
+    worked = (
+        jnp.einsum("ecf,efh->ech", hidden_act, expert_down, preferred_element_type=jnp.float32)
+        .astype(jnp.bfloat16)
+        .reshape(local_experts, owners, capacity, width)
+    )
     shared_hidden = (
         jax.nn.silu(jnp.dot(normed_all, shared_gate, preferred_element_type=jnp.float32))
         * jnp.dot(normed_all, shared_up, preferred_element_type=jnp.float32)
     ).astype(jnp.bfloat16)
-    ffn_term = routed + jnp.dot(shared_hidden, shared_down, preferred_element_type=jnp.float32)
-    ffn_own = lax.psum_scatter(
-        ffn_term.astype(jnp.bfloat16), "attn", scatter_dimension=0, tiled=True
-    ).astype(jnp.float32)
-    layer_out = (hidden_own + ffn_own).astype(jnp.bfloat16)[None]
+    shared_term = jnp.dot(shared_hidden, shared_down, preferred_element_type=jnp.float32)
+    partial = jnp.einsum(
+        "gesr,egsd->grd", picks, worked, preferred_element_type=jnp.float32
+    ).astype(jnp.bfloat16)
+    group_sum = lax.psum_scatter(partial, "expert", scatter_dimension=0, tiled=False)
+    ffn_term = (group_sum.astype(jnp.float32) + shared_term).astype(jnp.bfloat16)
+    ffn_own = lax.psum_scatter(ffn_term, "attn", scatter_dimension=0, tiled=True)
+    layer_out = (hidden_own + ffn_own.astype(jnp.float32)).astype(jnp.bfloat16)[None]
     return (layer_out, latent_out[None], rope_out[None])
 
 

time: 712 us -> 540 us (0.76)
  blocking collectives: 165 us -> 9.36 us
  waiting for transfers between devices: 264 us -> 360 us
  local copies, waits for them, and re-layouts: 104 us -> 24 us
  other arithmetic: 87.5 us -> 17.6 us
  matrix products: 66.7 us -> 114 us
    all_to_all x1 -> x0, blocking collectives: 165 us -> none  [local(): lax.all_to_all(outgoing, 'expert', split_axis=0, concat_axis=0, tiled=True)]
    reduce_scatter x1 -> x3, waiting for transfers between devices: 30.8 us -> 188 us  [the longest x1 112 us: local(): lax.psum_scatter(partial, 'expert', scatter_dimension=0, tiled=False)]
    all_to_all x1 -> x0, waiting for transfers between devices: 156 us -> none  [local(): lax.all_to_all(worked, 'expert', split_axis=0, concat_axis=0, tiled=True)]
    all_gather x0 -> x2, waiting for transfers between devices: none -> 126 us  [the longest x1 80.6 us: local(): rows_all = lax.all_gather(normed_all, 'expert', axis=0)]
    psum x1 -> x0, waiting for transfers between devices: 72.6 us -> none  [local(): lax.psum(term_all.astype(jnp.bfloat16), 'attn').astype(jnp.float32)]
    gather x3 -> x0, local copies, waits for them, and re-layouts: 65.8 us -> none  [the longest x2 51.2 us: local(): jnp.take(returned, target, axis=0).astype(jnp.float32)]
    dot_general x3 -> x6, matrix products: 39.6 us -> 85.3 us  [the longest x1 24.6 us: local(): jnp.einsum('ecf,efh->ech', hidden_act, expert_down, preferred_element_typ...]
    all_gather x1, waiting for transfers between devices: 4.64 us -> 45.2 us  [local(): piece = lax.all_gather(normed_own, 'attn', axis=0, tiled=True)]
  transfers between devices with their start and end apart: 4 -> 6, of which waited for: 4 -> 6; matrix products, arithmetic and copies ran while one was open for 10% -> 3% of each run, Pallas kernels for 0% -> 0%
where the time goes in v1:
time: 540 us; the launch traced here: 539 us
  waiting for transfers between devices  360 us (67%)
  matrix products  114 us (21%)
  local copies, waits for them, and re-layouts  24 us (4%)
  other arithmetic  17.6 us (3%)
  between operations  14.4 us (3%)
  blocking collectives  9.36 us (2%)
    reduce_scatter x1, waiting for transfers between devices, local(): lax.psum_scatter(partial, 'expert', scatter_dimension=0, tiled=False)  112 us
    all_gather x1, waiting for transfers between devices, local(): rows_all = lax.all_gather(normed_all, 'expert', axis=0)  80.6 us
    all_gather x1, waiting for transfers between devices, local(): normed_all = lax.all_gather(normed_ffn, 'attn', axis=0, tiled=True)  45.4 us
    all_gather x1, waiting for transfers between devices, local(): piece = lax.all_gather(normed_own, 'attn', axis=0, tiled=True)  45.2 us
    reduce_scatter x1, waiting for transfers between devices, local(): lax.psum_scatter(term_all.astype(jnp.bfloat16), 'attn', scatter_dimension...  42.6 us
    reduce_scatter x1, waiting for transfers between devices, local(): lax.psum_scatter(ffn_term, 'attn', scatter_dimension=0, tiled=True)  33.6 us
    dot_general x1, matrix products, local(): jnp.einsum('ecf,efh->ech', hidden_act, expert_down, preferred_element_typ...  24.6 us
    dot_general x1, matrix products, local(): jnp.einsum('gesr,grd->egsd', picks, rows_all, preferred_element_type=jnp....  17.7 us
  transfers between devices with their start and end apart: 6, of which 6 were waited for; matrix products, arithmetic and copies ran while one was open for 3% of the time, Pallas kernels for 0%

profile of v1, /device:TPU:0, one launch (start us, length us, event | category | flops | bytes accessed | tf_op | source)
XLA Modules:
  0.0 539.2 jit_solution(5349978278555513483)
XLA Ops:
  7.2 0.0 all-gather.5.cloned.1.call-start
  7.2 1.4 fusion.17
  8.6 0.7 convert_element_type.103
  9.3 2.0 fusion.19
  11.4 0.0 reduce-scatter.4.cloned.1.call-start
  11.4 0.7 copy.93
  12.1 0.7 convert_element_type.105
  12.8 0.3 fusion.33
  13.1 0.9 select_reduce_fusion.3
  13.9 0.1 convert_reduce_fusion
  14.0 0.7 fusion.36
  14.7 0.1 select_reduce_fusion.1
  14.8 0.2 fusion.20
  15.0 45.2 %all-gather.5.cloned.1.call-done = bf16[512,2048]{1,0:T(8,128)(2,1)} async-done(((bf16[128,2048]{1,0:T(8,128)(2,1)}), bf16[512,2048]{1,0:T(8,128)(2,1)}) %all-gather.5.cloned.1.call-update) | async-done | bytes 2097168 | tf_op jit(solution)/shard_map/all_gather | solution.py:116
  60.2 3.8 fusion.42
  64.0 0.1 multiply_reduce_fusion.1
  64.1 0.2 multiply_convert_fusion.3
  64.3 0.5 convolution_convert_fusion.2
  64.8 0.3 copy-done.3
  65.0 1.3 convolution_convert_fusion.3
  66.3 0.3 subtract_convert_fusion.1
  66.7 1.8 fusion.43
  68.5 0.8 fusion.24
  69.3 0.1 subtract_convert_fusion
  69.4 3.3 fusion.5
  72.6 5.2 fusion.14
  77.8 3.7 convolution_convert_fusion.1
  81.6 0.0 all-gather.7.cloned.1.call-start
  81.7 42.6 %reduce-scatter.4.cloned.1.call-done = bf16[128,2048]{1,0:T(8,128)(2,1)} async-done(((bf16[512,2048]{1,0:T(8,128)(2,1)}), bf16[128,2048]{1,0:T(8,128)(2,1)}) %reduce-scatter.4.cloned.1.call-update) | async-done | bytes 524304 | tf_op jit(solution)/shard_map/reduce_scatter | solution.py:181
  124.3 1.3 multiply_reduce_fusion
  125.6 2.0 multiply_convert_fusion.2
  127.7 0.0 all-gather.9.cloned.1.call-start
  127.7 45.4 %all-gather.7.cloned.1.call-done = bf16[512,2048]{1,0:T(8,128)(2,1)} async-done(((bf16[128,2048]{1,0:T(8,128)(2,1)}), bf16[512,2048]{1,0:T(8,128)(2,1)}) %all-gather.7.cloned.1.call-update) | async-done | bytes 2097168 | tf_op jit(solution)/shard_map/all_gather | solution.py:186
  173.2 9.4 %all_gather.16 = s32[8,512,6]{1,2,0:T(8,128)S(1)} all-gather(s32[1,512,6]{1,2,0:T(8,128)S(1)} %copy.75), channel_id=1, replica_groups=mesh['attn'=4,'expert'=8] {'expert'}, dimensions={0}, use_global_device_ids=true | all-gather | bytes 110592 | tf_op jit(solution)/shard_map/all_gather | solution.py:112
  182.6 0.2 compare_reduce_fusion
  182.7 0.2 fusion.16
  183.0 0.1 copy.77
  183.1 80.6 %all-gather.9.cloned.1.call-done = bf16[4096,2048]{1,0:T(8,128)(2,1)} async-done(((bf16[512,2048]{1,0:T(8,128)(2,1)}), bf16[4096,2048]{1,0:T(8,128)(2,1)}) %all-gather.9.cloned.1.call-update) | async-done | bytes 16777232 | tf_op jit(solution)/shard_map/all_gather | solution.py:187
  263.6 11.0 %fusion.41 = (f32[8,512]{1,0:T(8,128)S(1)}, f32[8,512,64]{1,2,0:T(8,128)S(1)}) fusion(bf16[8,512,2048]{2,1,0:T(8,128)(2,1)} %bitcast.96, bf16[2048,64]{0,1:T(8,128)(2,1)S(1)} %copy-done.8), kind=kOutput, calls=%fused_computation.105 | convolution fusion | flops 1073999872 | bytes 18104320 | tf_op jit(solution)/shard_map/grd,dx->grx/dot_general | solution.py:192
  274.6 0.1 copy.78
  274.7 1.3 select_reduce_fusion
  276.0 0.1 mul.206
  276.1 17.7 %convert_bitcast_fusion = bf16[8,8,56,2048]{3,2,0,1:T(8,128)(2,1)} fusion(bf16[8,512,2048,1]{2,1,3,0:T(8,128)(2,1)} %bitcast.97, s32[8,8,512]{2,1,0:T(8,128)S(1)} %fusion.16), kind=kOutput, calls=%fused_computation.4 | convolution fusion | flops 7525367808 | bytes 31588352 | tf_op jit(solution)/shard_map/gesr,grd->egsd/dot_general | solution.py:201
  293.8 13.5 %copy.76 = bf16[8,8,56,2048]{3,2,1,0:T(8,128)(2,1)} copy(bf16[8,8,56,2048]{3,2,0,1:T(8,128)(2,1)} %convert_bitcast_fusion) | data formatting | bytes 29360128 | tf_op jit(solution)/shard_map/convert_element_type | solution.py:202
  307.3 16.4 %fusion.44 = f32[8,448,352]{2,1,0:T(8,128)} fusion(bf16[8,448,2048]{2,1,0:T(8,128)(2,1)} %bitcast.98, bf16[8,2048,352]{1,2,0:T(8,128)(2,1)} %param.32), kind=kOutput, calls=%fused_computation.108 | convolution fusion | flops 5167382528 | bytes 31260672 | tf_op jit(solution)/shard_map/ech,ehf->ecf/dot_general | solution.py:205
  323.7 24.6 %convolution_convert_fusion = bf16[8,448,2048]{2,1,0:T(8,128)(2,1)} fusion(bf16[8,352,2048]{2,1,0:T(8,128)(2,1)} %param.34, f32[8,448,352]{2,1,0:T(8,128)} %fusion.44, bf16[8,448,2048]{2,1,0:T(8,128)(2,1)} %bitcast.99, bf16[8,2048,352]{1,2,0:T(8,128)(2,1)} %param.33, f32[8,448]{1,0:T(8,128)S(1)} %mul.206), kind=kOutput, calls=%fused_computation.5 | convolution fusion | flops 10350936064 | bytes 57489408 | tf_op jit(solution)/shard_map/ecf,efh->ech/dot_general | solution.py:209
  348.3 15.5 %bitcast_convert_fusion = bf16[8,512,2048]{2,1,0:T(8,128)(2,1)} fusion(bf16[8,8,56,2048]{3,2,1,0:T(8,128)(2,1)} %bitcast.109, s32[8,8,512]{2,1,0:T(8,128)S(1)} %fusion.16), kind=kOutput, calls=%fused_computation.2 | convolution fusion | flops 7526416384 | bytes 31588352 | tf_op jit(solution)/shard_map/gesr,egsd->grd/dot_general | solution.py:218
  363.8 0.0 reduce-scatter.8.cloned.1.call-start
  363.8 1.5 copy-done.4
  365.4 2.3 fusion.45
  367.7 112.2 %reduce-scatter.6.cloned.1.call-done = bf16[1,512,2048]{2,1,0:T(8,128)(2,1)} async-done(((bf16[8,512,2048]{2,1,0:T(8,128)(2,1)}), bf16[1,512,2048]{2,1,0:T(8,128)(2,1)}) %reduce-scatter.6.cloned.1.call-update) | async-done | bytes 2097168 | tf_op jit(solution)/shard_map/reduce_scatter | solution.py:221
  479.9 6.0 %fusion.2 = bf16[512,2048]{1,0:T(8,128)(2,1)} fusion(bf16[352,2048]{1,0:T(8,128)(2,1)} %param.37, bf16[1,512,2048]{2,1,0:T(8,128)(2,1)} %reduce-scatter.6.cloned.1.call-done, bf16[512,2048]{1,0:T(8,128)(2,1)S(1)} %copy-done.4, bf16[2048,352]{0,1:T(8,128)(2,1)} %param.36, f32[512,352]{0,1:T(8,128)S(1)} %fusion.45), kind=kOutput, calls=%fused_computation.12 | convolution fusion | flops 1480622080 | bytes 9895936 | tf_op jit(solution)/shard_map/dot_general | solution.py:217
  485.9 0.2 select_reduce_fusion.2
  486.1 0.1 fusion.34
  486.2 0.1 fusion.35
  486.3 2.2 copy.80
  488.5 0.1 copy.81
  488.6 1.4 gather_fusion.1
  490.1 0.7 copy.82
  490.8 3.2 gather_fusion
  494.0 1.4 select_bitcast_fusion
  495.4 0.9 select_select_fusion
  496.4 33.6 %reduce-scatter.8.cloned.1.call-done = bf16[128,2048]{1,0:T(8,128)(2,1)} async-done(((bf16[512,2048]{1,0:T(8,128)(2,1)}), bf16[128,2048]{1,0:T(8,128)(2,1)}) %reduce-scatter.8.cloned.1.call-update) | async-done | bytes 524304 | tf_op jit(solution)/shard_map/reduce_scatter | solution.py:223
  529.9 2.4 fusion.23
  (44 shorter events, 0.3 us)
Async XLA Ops:
  7.2 59.5 %copy-start = (bf16[2048,768]{1,0:T(8,128)(2,1)S(1)}, bf16[2048,768]{1,0:T(8,128)(2,1)}, u32[]{:S(2)}) copy-start(bf16[2048,768]{1,0:T(8,128)(2,1)} %param.24) | copy-start | bytes 9437188
  7.2 53.0 %all-gather.5.cloned.1.call-start = ((), (), s32[]{:S(2)}) async-start(), calls=%async_computation.3 | async-start | bytes 2621440 | tf_op jit(solution)/shard_map/all_gather | solution.py:116
  11.4 113.0 %reduce-scatter.4.cloned.1.call-start = ((), (), s32[]{:S(2)}) async-start(), calls=%async_computation.4 | async-start | bytes 2621440 | tf_op jit(solution)/shard_map/reduce_scatter | solution.py:181
  60.2 4.1 copy-start.5
  63.9 1.1 copy-start.6
  63.9 2.7 copy-start.12
  64.3 0.8 copy-start.3
  69.4 3.3 copy-start.7
  72.6 5.2 copy-start.11
  77.8 3.8 copy-start.10
  77.8 46.5 %copy-start.2 = (bf16[1,128,2048]{2,1,0:T(8,128)(2,1)S(1)}, bf16[1,128,2048]{2,1,0:T(8,128)(2,1)}, u32[]{:S(2)}) copy-start(bf16[1,128,2048]{2,1,0:T(8,128)(2,1)} %param.19) | copy-start | bytes 1572868
  81.6 91.6 %copy-start.9 = (s32[1,512,6]{1,0,2:T(1,128)S(1)}, s32[1,512,6]{1,0,2:T(1,128)}, u32[]{:S(2)}) copy-start(s32[1,512,6]{1,0,2:T(1,128)} %param.22) | copy-start | bytes 36868
  81.6 182.1 %copy-start.8 = (bf16[2048,64]{0,1:T(8,128)(2,1)S(1)}, bf16[2048,64]{0,1:T(8,128)(2,1)}, u32[]{:S(2)}) copy-start(bf16[2048,64]{0,1:T(8,128)(2,1)} %param.31) | copy-start | bytes 786436
  81.6 91.5 %all-gather.7.cloned.1.call-start = ((), (), s32[]{:S(2)}) async-start(), calls=%async_computation.5 | async-start | bytes 2621440 | tf_op jit(solution)/shard_map/all_gather | solution.py:186
  127.7 135.9 %all-gather.9.cloned.1.call-start = ((), (), s32[]{:S(2)}) async-start(), calls=%async_computation.8 | async-start | bytes 18874368 | tf_op jit(solution)/shard_map/all_gather | solution.py:187
  173.1 306.8 %reduce-scatter.6.cloned.1.call-start = ((), (), s32[]{:S(2)}) async-start(), calls=%async_computation.6 | async-start | bytes 18874368 | tf_op jit(solution)/shard_map/reduce_scatter | solution.py:221
  363.8 1.6 copy-start.4
  363.8 166.2 %reduce-scatter.8.cloned.1.call-start = ((), (), s32[]{:S(2)}) async-start(), calls=%async_computation.7 | async-start | bytes 2621440 | tf_op jit(solution)/shard_map/reduce_scatter | solution.py:223
  486.3 46.0 %copy-start.1 = (bf16[2048,768]{1,0:T(8,128)(2,1)S(1)}, bf16[2048,768]{1,0:T(8,128)(2,1)}, u32[]{:S(2)}) copy-start(bf16[2048,768]{1,0:T(8,128)(2,1)} %param.24) | copy-start | bytes 9437188
Sparse Core Ops, SparseCore 0:
  11.5 48.6 all-gather.4
  81.7 42.5 reduce-scatter.3
  127.8 45.2 all-gather.6
  175.0 88.5 all-gather.8
  363.9 115.9 reduce-scatter.5
  486.1 43.8 reduce-scatter.7

commit v2 on v1

--- a/solution.py
+++ b/solution.py
@@ -183,9 +183,12 @@
     ).astype(jnp.float32)
     hidden_own = residual_own + attn_own
     normed_ffn = rms_apply(hidden_own, ffn_gain).astype(jnp.bfloat16)
-    normed_all = lax.all_gather(normed_ffn, "attn", axis=0, tiled=True)
-    rows_all = lax.all_gather(normed_all, "expert", axis=0)
-    width = normed_all.shape[1]
+    width = normed_ffn.shape[1]
+    rows_all = lax.all_gather(normed_ffn, ("expert", "attn"), axis=0, tiled=True).reshape(
+        owners, group_rows, width
+    )
+    own_group = lax.axis_index("expert")
+    normed_all = lax.dynamic_index_in_dim(rows_all, own_group, 0, keepdims=False)
 
     picks = pick_matrix(routes_all, first_expert, local_experts, capacity)
 
@@ -215,12 +218,17 @@
         * jnp.dot(normed_all, shared_up, preferred_element_type=jnp.float32)
     ).astype(jnp.bfloat16)
     shared_term = jnp.dot(shared_hidden, shared_down, preferred_element_type=jnp.float32)
-    partial = jnp.einsum(
-        "gesr,egsd->grd", picks, worked, preferred_element_type=jnp.float32
+    group_ids = jnp.arange(owners, dtype=jnp.int32)[:, None, None]
+    partial = (
+        jnp.einsum("gesr,egsd->grd", picks, worked, preferred_element_type=jnp.float32)
+        + jnp.where(group_ids == own_group, shared_term[None], 0.0)
     ).astype(jnp.bfloat16)
-    group_sum = lax.psum_scatter(partial, "expert", scatter_dimension=0, tiled=False)
-    ffn_term = (group_sum.astype(jnp.float32) + shared_term).astype(jnp.bfloat16)
-    ffn_own = lax.psum_scatter(ffn_term, "attn", scatter_dimension=0, tiled=True)
+    ffn_own = lax.psum_scatter(
+        partial.reshape(owners * group_rows, width),
+        ("expert", "attn"),
+        scatter_dimension=0,
+        tiled=True,
+    )
     layer_out = (hidden_own + ffn_own.astype(jnp.float32)).astype(jnp.bfloat16)[None]
     return (layer_out, latent_out[None], rope_out[None])
 

time: 540 us -> 729 us (1.35)
  waiting for transfers between devices: 360 us -> 545 us
    reduce_scatter x2 -> x1, waiting for transfers between devices: 146 us -> 352 us  [local(): lax.psum_scatter(partial.reshape(owners * group_rows, width), ('expert',...]
    all_gather x2 -> x1, waiting for transfers between devices: 126 us -> 105 us  [local(): lax.all_gather(normed_ffn, ('expert', 'attn'), axis=0, tiled=True)]
  transfers between devices with their start and end apart: 6 -> 4, of which waited for: 6 -> 4; matrix products, arithmetic and copies ran while one was open for 3% -> 2% of each run, Pallas kernels for 0% -> 0%
where the time goes in v2:
time: 729 us; the launch traced here: 728 us
  waiting for transfers between devices  545 us (75%)
  matrix products  120 us (16%)
  local copies, waits for them, and re-layouts  22.6 us (3%)
  other arithmetic  17.6 us (2%)
  between operations  14 us (2%)
  blocking collectives  9.36 us (1%)
    reduce_scatter x1, waiting for transfers between devices, local(): lax.psum_scatter(partial.reshape(owners * group_rows, width), ('expert',...  352 us
    all_gather x1, waiting for transfers between devices, local(): lax.all_gather(normed_ffn, ('expert', 'attn'), axis=0, tiled=True)  105 us
    all_gather x1, waiting for transfers between devices, local(): piece = lax.all_gather(normed_own, 'attn', axis=0, tiled=True)  45.2 us
    reduce_scatter x1, waiting for transfers between devices, local(): lax.psum_scatter(term_all.astype(jnp.bfloat16), 'attn', scatter_dimension...  42.7 us
    dot_general x1, matrix products, local(): jnp.einsum('ecf,efh->ech', hidden_act, expert_down, preferred_element_typ...  24.5 us
    dot_general x1, matrix products, local(): jnp.einsum('gesr,egsd->grd', picks, worked, preferred_element_type=jnp.fl...  20.5 us
    dot_general x1, matrix products, local(): jnp.einsum('gesr,grd->egsd', picks, rows_all, preferred_element_type=jnp....  17.8 us
    dot_general x1, matrix products, local(): jnp.einsum('ech,ehf->ecf', arrived, expert_gate, preferred_element_type=j...  16.5 us
  transfers between devices with their start and end apart: 4, of which 4 were waited for; matrix products, arithmetic and copies ran while one was open for 2% of the time, Pallas kernels for 0%

profile of v2, /device:TPU:0, one launch (start us, length us, event | category | flops | bytes accessed | tf_op | source)
XLA Modules:
  0.0 728.3 jit_solution(7123665297272738316)
XLA Ops:
  7.2 0.0 all-gather.3.cloned.1.call-start
  7.2 1.4 fusion.31
  8.6 0.7 convert_element_type.94
  9.3 2.0 fusion.33
  11.3 0.0 all-gather.3.cloned.1.call-update
  11.4 0.0 reduce-scatter.3.cloned.1.call-start
  11.4 0.7 copy.93
  12.1 0.7 convert_element_type.96
  12.8 0.3 fusion.52
  13.1 0.9 select_reduce_fusion.3
  13.9 0.1 convert_reduce_fusion
  14.0 0.7 fusion.55
  14.7 0.1 select_reduce_fusion.1
  14.8 0.2 fusion.34
  15.0 45.2 %all-gather.3.cloned.1.call-done = bf16[512,2048]{1,0:T(8,128)(2,1)} async-done(((bf16[128,2048]{1,0:T(8,128)(2,1)}), bf16[512,2048]{1,0:T(8,128)(2,1)}) %all-gather.3.cloned.1.call-update) | async-done | bytes 2097168 | tf_op jit(solution)/shard_map/all_gather | solution.py:116
  60.2 3.8 fusion.64
  64.0 0.1 multiply_reduce_fusion.1
  64.1 0.2 multiply_convert_fusion.3
  64.3 0.5 convolution_convert_fusion.2
  64.8 0.3 copy-done.3
  65.0 1.3 convolution_convert_fusion.3
  66.3 0.3 subtract_convert_fusion.1
  66.7 1.8 fusion.65
  68.5 0.8 fusion.43
  69.3 0.1 subtract_convert_fusion
  69.4 3.3 fusion.5
  72.6 5.2 fusion.20
  77.8 3.7 convolution_convert_fusion.1
  81.6 0.0 reduce-scatter.3.cloned.1.call-update
  81.6 0.0 all-gather.5.cloned.1.call-start
  81.7 42.7 %reduce-scatter.3.cloned.1.call-done = bf16[128,2048]{1,0:T(8,128)(2,1)} async-done(((bf16[512,2048]{1,0:T(8,128)(2,1)}), bf16[128,2048]{1,0:T(8,128)(2,1)}) %reduce-scatter.3.cloned.1.call-update) | async-done | bytes 524304 | tf_op jit(solution)/shard_map/reduce_scatter | solution.py:181
  124.3 1.3 multiply_reduce_fusion
  125.7 2.0 multiply_convert_fusion.2
  127.7 0.0 all-gather.5.cloned.1.call-update
  127.7 0.0 reduce-scatter.5.cloned.1.call-start
  127.8 9.4 %all_gather.10 = s32[8,512,6]{1,2,0:T(8,128)S(1)} all-gather(s32[1,512,6]{1,2,0:T(8,128)S(1)} %copy.75), channel_id=1, replica_groups=mesh['attn'=4,'expert'=8] {'expert'}, dimensions={0}, use_global_device_ids=true | all-gather | bytes 110592 | tf_op jit(solution)/shard_map/all_gather | solution.py:112
  137.2 0.2 compare_reduce_fusion
  137.3 0.2 fusion.30
  137.5 0.1 copy.77
  137.6 105.0 %all-gather.5.cloned.1.call-done = bf16[4096,2048]{1,0:T(8,128)(2,1)} async-done(((bf16[128,2048]{1,0:T(8,128)(2,1)}), bf16[4096,2048]{1,0:T(8,128)(2,1)}) %all-gather.5.cloned.1.call-update) | async-done | bytes 16777232 | tf_op jit(solution)/shard_map/all_gather | solution.py:187
  242.6 11.0 %fusion.63 = (f32[8,512]{1,0:T(8,128)S(1)}, f32[8,512,64]{1,2,0:T(8,128)S(1)}) fusion(bf16[8,512,2048]{2,1,0:T(8,128)(2,1)} %bitcast.105, bf16[2048,64]{0,1:T(8,128)(2,1)S(1)} %copy-done.7), kind=kOutput, calls=%fused_computation.119 | convolution fusion | flops 1073999872 | bytes 18104320 | tf_op jit(solution)/shard_map/grd,dx->grx/dot_general | solution.py:195
  253.6 0.1 copy.78
  253.7 1.3 select_reduce_fusion
  255.0 0.1 mul.206
  255.1 17.8 %convert_bitcast_fusion = bf16[8,8,56,2048]{3,2,0,1:T(8,128)(2,1)} fusion(bf16[8,512,2048,1]{2,1,3,0:T(8,128)(2,1)} %bitcast.106, s32[8,8,512]{2,1,0:T(8,128)S(1)} %fusion.30), kind=kOutput, calls=%fused_computation.5 | convolution fusion | flops 7525367808 | bytes 31588352 | tf_op jit(solution)/shard_map/gesr,grd->egsd/dot_general | solution.py:204
  272.9 13.6 %copy.76 = bf16[8,8,56,2048]{3,2,1,0:T(8,128)(2,1)} copy(bf16[8,8,56,2048]{3,2,0,1:T(8,128)(2,1)} %convert_bitcast_fusion) | data formatting | bytes 29360128 | tf_op jit(solution)/shard_map/convert_element_type | solution.py:205
  286.5 2.5 fusion.14
  289.0 16.5 %fusion.66 = f32[8,448,352]{2,1,0:T(8,128)} fusion(bf16[8,448,2048]{2,1,0:T(8,128)(2,1)} %bitcast.110, bf16[8,2048,352]{1,2,0:T(8,128)(2,1)} %param.32), kind=kOutput, calls=%fused_computation.122 | convolution fusion | flops 5167382528 | bytes 31260672 | tf_op jit(solution)/shard_map/ech,ehf->ecf/dot_general | solution.py:208
  305.6 6.3 fusion.28
  311.8 24.5 %convolution_convert_fusion = bf16[8,448,2048]{2,1,0:T(8,128)(2,1)} fusion(bf16[8,352,2048]{2,1,0:T(8,128)(2,1)} %param.34, f32[8,448,352]{2,1,0:T(8,128)} %fusion.66, bf16[8,448,2048]{2,1,0:T(8,128)(2,1)} %bitcast.111, bf16[8,2048,352]{1,2,0:T(8,128)(2,1)} %param.33, f32[8,448]{1,0:T(8,128)S(1)} %mul.206), kind=kOutput, calls=%fused_computation.6 | convolution fusion | flops 10350936064 | bytes 57489408 | tf_op jit(solution)/shard_map/ecf,efh->ech/dot_general | solution.py:212
  336.3 20.5 %fusion = bf16[8,512,2048]{2,1,0:T(8,128)(2,1)} fusion(f32[512,2048]{1,0:T(8,128)} %fusion.28, pred[8]{0:T(512)(128)(4,1)S(1)} %iota_compare_fusion.10, bf16[8,8,56,2048]{3,2,1,0:T(8,128)(2,1)} %bitcast.121, s32[8,8,512]{2,1,0:T(8,128)S(1)} %fusion.30), kind=kOutput, calls=%fused_computation.3 | convolution fusion | flops 7543193600 | bytes 35782664 | tf_op jit(solution)/shard_map/gesr,egsd->grd/dot_general | solution.py:223
  356.8 0.0 reduce-scatter.5.cloned.1.call-update
  356.8 0.2 select_reduce_fusion.2
  357.0 0.1 fusion.53
  357.1 0.1 fusion.54
  357.2 2.2 copy.80
  359.4 0.1 copy.81
  359.5 1.4 gather_fusion.1
  361.0 0.7 copy.82
  361.7 3.2 gather_fusion
  364.9 1.4 select_bitcast_fusion
  366.3 0.9 select_select_fusion
  367.3 352.1 %reduce-scatter.5.cloned.1.call-done = bf16[128,2048]{1,0:T(8,128)(2,1)} async-done(((bf16[4096,2048]{1,0:T(8,128)(2,1)}), bf16[128,2048]{1,0:T(8,128)(2,1)}) %reduce-scatter.5.cloned.1.call-update) | async-done | bytes 524304 | tf_op jit(solution)/shard_map/reduce_scatter | solution.py:226
  719.4 2.4 fusion.42
  (41 shorter events, 0.2 us)
Async XLA Ops:
  7.2 59.5 %copy-start = (bf16[2048,768]{1,0:T(8,128)(2,1)S(1)}, bf16[2048,768]{1,0:T(8,128)(2,1)}, u32[]{:S(2)}) copy-start(bf16[2048,768]{1,0:T(8,128)(2,1)} %param.24) | copy-start | bytes 9437188
  7.2 53.0 %all-gather.3.cloned.1.call-start = ((), (), s32[]{:S(2)}) async-start(), calls=%async_computation.2 | async-start | bytes 2621440 | tf_op jit(solution)/shard_map/all_gather | solution.py:116
  11.4 113.0 %reduce-scatter.3.cloned.1.call-start = ((), (), s32[]{:S(2)}) async-start(), calls=%async_computation.3 | async-start | bytes 2621440 | tf_op jit(solution)/shard_map/reduce_scatter | solution.py:181
  60.2 4.1 copy-start.4
  63.9 1.1 copy-start.5
  63.9 2.7 copy-start.11
  64.3 0.8 copy-start.3
  69.4 3.3 copy-start.6
  72.6 5.2 copy-start.10
  77.8 3.8 copy-start.9
  77.8 46.5 %copy-start.2 = (bf16[1,128,2048]{2,1,0:T(8,128)(2,1)S(1)}, bf16[1,128,2048]{2,1,0:T(8,128)(2,1)}, u32[]{:S(2)}) copy-start(bf16[1,128,2048]{2,1,0:T(8,128)(2,1)} %param.19) | copy-start | bytes 1572868
  77.8 50.0 %copy-start.8 = (s32[1,512,6]{1,0,2:T(1,128)S(1)}, s32[1,512,6]{1,0,2:T(1,128)}, u32[]{:S(2)}) copy-start(s32[1,512,6]{1,0,2:T(1,128)} %param.22) | copy-start | bytes 36868
  81.6 161.0 %copy-start.7 = (bf16[2048,64]{0,1:T(8,128)(2,1)S(1)}, bf16[2048,64]{0,1:T(8,128)(2,1)}, u32[]{:S(2)}) copy-start(bf16[2048,64]{0,1:T(8,128)(2,1)} %param.31) | copy-start | bytes 786436
  81.6 161.0 %all-gather.5.cloned.1.call-start = ((), (), s32[]{:S(2)}) async-start(), calls=%async_computation.4 | async-start | bytes 17301504 | tf_op jit(solution)/shard_map/all_gather | solution.py:187
  127.7 591.6 %reduce-scatter.5.cloned.1.call-start = ((), (), s32[]{:S(2)}) async-start(), calls=%async_computation.5 | async-start | bytes 17301504 | tf_op jit(solution)/shard_map/reduce_scatter | solution.py:226
  272.9 13.6 %copy-start.12 = (bf16[2048,352]{0,1:T(8,128)(2,1)S(1)}, bf16[2048,352]{0,1:T(8,128)(2,1)}, u32[]{:S(2)}) copy-start(bf16[2048,352]{0,1:T(8,128)(2,1)} %param.35) | copy-start | bytes 4325380
  289.0 16.5 %copy-start.13 = (bf16[352,2048]{1,0:T(8,128)(2,1)S(1)}, bf16[352,2048]{1,0:T(8,128)(2,1)}, u32[]{:S(2)}) copy-start(bf16[352,2048]{1,0:T(8,128)(2,1)} %param.37) | copy-start | bytes 4325380
  357.2 364.6 %copy-start.1 = (bf16[2048,768]{1,0:T(8,128)(2,1)S(1)}, bf16[2048,768]{1,0:T(8,128)(2,1)}, u32[]{:S(2)}) copy-start(bf16[2048,768]{1,0:T(8,128)(2,1)} %param.24) | copy-start | bytes 9437188
Sparse Core Ops, SparseCore 0:
  11.5 48.6 all-gather.2
  81.7 42.5 reduce-scatter.2
  128.4 114.1 all-gather.4
  357.0 362.3 reduce-scatter.4

commit v3 on v1

--- a/solution.py
+++ b/solution.py
@@ -183,9 +183,12 @@
     ).astype(jnp.float32)
     hidden_own = residual_own + attn_own
     normed_ffn = rms_apply(hidden_own, ffn_gain).astype(jnp.bfloat16)
-    normed_all = lax.all_gather(normed_ffn, "attn", axis=0, tiled=True)
-    rows_all = lax.all_gather(normed_all, "expert", axis=0)
-    width = normed_all.shape[1]
+    width = normed_ffn.shape[1]
+    rows_all = lax.all_gather(normed_ffn, ("expert", "attn"), axis=0, tiled=True).reshape(
+        owners, group_rows, width
+    )
+    own_group = lax.axis_index("expert")
+    normed_all = lax.dynamic_index_in_dim(rows_all, own_group, 0, keepdims=False)
 
     picks = pick_matrix(routes_all, first_expert, local_experts, capacity)
 

time: 540 us -> 512 us (0.948)
  waiting for transfers between devices: 360 us -> 336 us
  matrix products: 114 us -> 108 us
    all_gather x2 -> x1, waiting for transfers between devices: 126 us -> 105 us  [local(): lax.all_gather(normed_ffn, ('expert', 'attn'), axis=0, tiled=True)]
    dot_general x1, matrix products: 11 us -> 5.2 us  [local(): jnp.einsum('grd,dx->grx', rows_all, w_router, preferred_element_type=jnp....]
  transfers between devices with their start and end apart: 6 -> 5, of which waited for: 6 -> 5; matrix products, arithmetic and copies ran while one was open for 3% -> 3% of each run, Pallas kernels for 0% -> 0%
where the time goes in v3:
time: 512 us; the launch traced here: 511 us
  waiting for transfers between devices  336 us (66%)
  matrix products  108 us (21%)
  local copies, waits for them, and re-layouts  26.3 us (5%)
  other arithmetic  17.7 us (3%)
  between operations  14.1 us (3%)
  blocking collectives  9.18 us (2%)
    reduce_scatter x1, waiting for transfers between devices, local(): lax.psum_scatter(partial, 'expert', scatter_dimension=0, tiled=False)  110 us
    all_gather x1, waiting for transfers between devices, local(): lax.all_gather(normed_ffn, ('expert', 'attn'), axis=0, tiled=True)  105 us
    all_gather x1, waiting for transfers between devices, local(): piece = lax.all_gather(normed_own, 'attn', axis=0, tiled=True)  45.2 us
    reduce_scatter x1, waiting for transfers between devices, local(): lax.psum_scatter(term_all.astype(jnp.bfloat16), 'attn', scatter_dimension...  42.6 us
    reduce_scatter x1, waiting for transfers between devices, local(): lax.psum_scatter(ffn_term, 'attn', scatter_dimension=0, tiled=True)  33.6 us
    dot_general x1, matrix products, local(): jnp.einsum('ecf,efh->ech', hidden_act, expert_down, preferred_element_typ...  24.5 us
    dot_general x1, matrix products, local(): jnp.einsum('gesr,grd->egsd', picks, rows_all, preferred_element_type=jnp....  17.5 us
    dot_general x1, matrix products, local(): jnp.einsum('ech,ehf->ecf', arrived, expert_gate, preferred_element_type=j...  16.4 us
  transfers between devices with their start and end apart: 5, of which 5 were waited for; matrix products, arithmetic and copies ran while one was open for 3% of the time, Pallas kernels for 0%

profile of v3, /device:TPU:0, one launch (start us, length us, event | category | flops | bytes accessed | tf_op | source)
XLA Modules:
  0.0 511.3 jit_solution(16029877365796877718)
XLA Ops:
  7.2 0.0 all-gather.3.cloned.1.call-start
  7.2 0.8 convert_element_type.103
  8.1 1.3 fusion.28
  9.4 2.0 fusion.30
  11.4 0.0 all-gather.3.cloned.1.call-update
  11.4 0.0 reduce-scatter.4.cloned.1.call-start
  11.5 0.7 copy.93
  12.2 0.7 convert_element_type.105
  12.9 0.3 fusion.49
  13.1 0.9 select_reduce_fusion.3
  14.0 0.1 convert_reduce_fusion
  14.1 0.7 fusion.52
  14.8 0.1 select_reduce_fusion.1
  14.9 0.2 fusion.31
  15.1 45.2 %all-gather.3.cloned.1.call-done = bf16[512,2048]{1,0:T(8,128)(2,1)} async-done(((bf16[128,2048]{1,0:T(8,128)(2,1)}), bf16[512,2048]{1,0:T(8,128)(2,1)}) %all-gather.3.cloned.1.call-update) | async-done | bytes 2097168 | tf_op jit(solution)/shard_map/all_gather | solution.py:116
  60.2 3.8 fusion.61
  64.0 0.1 multiply_reduce_fusion.1
  64.1 0.2 multiply_convert_fusion.3
  64.3 0.5 convolution_convert_fusion.2
  64.8 0.3 copy-done.4
  65.1 1.3 convolution_convert_fusion.3
  66.4 0.3 subtract_convert_fusion.1
  66.7 1.8 fusion.62
  68.6 0.7 fusion.40
  69.3 0.1 subtract_convert_fusion
  69.4 3.3 fusion.5
  72.7 4.4 fusion.20
  77.2 2.6 convolution_convert_fusion.1
  79.8 0.0 all-gather.5.cloned.1.call-start
  79.9 42.6 %reduce-scatter.4.cloned.1.call-done = bf16[128,2048]{1,0:T(8,128)(2,1)} async-done(((bf16[512,2048]{1,0:T(8,128)(2,1)}), bf16[128,2048]{1,0:T(8,128)(2,1)}) %reduce-scatter.4.cloned.1.call-update) | async-done | bytes 524304 | tf_op jit(solution)/shard_map/reduce_scatter | solution.py:181
  122.6 1.3 multiply_reduce_fusion
  123.9 2.0 multiply_convert_fusion.2
  125.9 0.0 reduce-scatter.6.cloned.1.call-start
  126.0 9.2 %all_gather.10 = s32[8,512,6]{1,2,0:T(8,128)S(1)} all-gather(s32[1,512,6]{1,2,0:T(8,128)S(1)} %copy.75), channel_id=1, replica_groups=mesh['attn'=4,'expert'=8] {'expert'}, dimensions={0}, use_global_device_ids=true | all-gather | bytes 110592 | tf_op jit(solution)/shard_map/all_gather | solution.py:112
  135.2 0.2 compare_reduce_fusion
  135.4 0.2 fusion.27
  135.6 0.1 copy.77
  135.7 105.2 %all-gather.5.cloned.1.call-done = bf16[4096,2048]{1,0:T(8,128)(2,1)} async-done(((bf16[128,2048]{1,0:T(8,128)(2,1)}), bf16[4096,2048]{1,0:T(8,128)(2,1)}) %all-gather.5.cloned.1.call-update) | async-done | bytes 16777232 | tf_op jit(solution)/shard_map/all_gather | solution.py:187
  240.8 17.5 %convert_bitcast_fusion = bf16[8,8,56,2048]{3,2,0,1:T(8,128)(2,1)} fusion(bf16[8,512,2048,1]{2,1,3,0:T(8,128)(2,1)} %bitcast.105, s32[8,8,512]{2,1,0:T(8,128)S(1)} %fusion.27), kind=kOutput, calls=%fused_computation.4 | convolution fusion | flops 7525367808 | bytes 31588352 | tf_op jit(solution)/shard_map/gesr,grd->egsd/dot_general | solution.py:204
  258.3 16.1 %copy.76 = bf16[8,8,56,2048]{3,2,1,0:T(8,128)(2,1)} copy(bf16[8,8,56,2048]{3,2,0,1:T(8,128)(2,1)} %convert_bitcast_fusion) | data formatting | bytes 29360128 | tf_op jit(solution)/shard_map/convert_element_type | solution.py:205
  274.4 5.2 %fusion.60 = (f32[8,512]{1,0:T(8,128)S(1)}, f32[8,512,64]{1,2,0:T(8,128)S(1)}) fusion(bf16[8,512,2048]{2,1,0:T(8,128)(2,1)S(1)} %bitcast.108, bf16[2048,64]{0,1:T(8,128)(2,1)S(1)} %copy-done.8), kind=kOutput, calls=%fused_computation.116 | convolution fusion | flops 1073999872 | bytes 18104320 | tf_op jit(solution)/shard_map/grd,dx->grx/dot_general | solution.py:195
  279.6 0.1 copy.78
  279.7 1.3 select_reduce_fusion
  281.0 0.1 mul.206
  281.1 16.4 %fusion.63 = f32[8,448,352]{2,1,0:T(8,128)} fusion(bf16[8,448,2048]{2,1,0:T(8,128)(2,1)} %bitcast.109, bf16[8,2048,352]{1,2,0:T(8,128)(2,1)} %param.32), kind=kOutput, calls=%fused_computation.119 | convolution fusion | flops 5167382528 | bytes 31260672 | tf_op jit(solution)/shard_map/ech,ehf->ecf/dot_general | solution.py:208
  297.5 24.5 %convolution_convert_fusion = bf16[8,448,2048]{2,1,0:T(8,128)(2,1)} fusion(bf16[8,352,2048]{2,1,0:T(8,128)(2,1)} %param.34, f32[8,448,352]{2,1,0:T(8,128)} %fusion.63, bf16[8,448,2048]{2,1,0:T(8,128)(2,1)} %bitcast.110, bf16[8,2048,352]{1,2,0:T(8,128)(2,1)} %param.33, f32[8,448]{1,0:T(8,128)S(1)} %mul.206), kind=kOutput, calls=%fused_computation.5 | convolution fusion | flops 10350936064 | bytes 57489408 | tf_op jit(solution)/shard_map/ecf,efh->ech/dot_general | solution.py:212
  322.1 15.5 %bitcast_convert_fusion = bf16[8,512,2048]{2,1,0:T(8,128)(2,1)} fusion(bf16[8,8,56,2048]{3,2,1,0:T(8,128)(2,1)} %bitcast.120, s32[8,8,512]{2,1,0:T(8,128)S(1)} %fusion.27), kind=kOutput, calls=%fused_computation.2 | convolution fusion | flops 7526416384 | bytes 31588352 | tf_op jit(solution)/shard_map/gesr,egsd->grd/dot_general | solution.py:221
  337.6 0.0 reduce-scatter.8.cloned.1.call-start
  337.7 1.3 copy-done.13
  338.9 3.4 fusion.14
  342.4 109.5 %reduce-scatter.6.cloned.1.call-done = bf16[1,512,2048]{2,1,0:T(8,128)(2,1)} async-done(((bf16[8,512,2048]{2,1,0:T(8,128)(2,1)}), bf16[1,512,2048]{2,1,0:T(8,128)(2,1)}) %reduce-scatter.6.cloned.1.call-update) | async-done | bytes 2097168 | tf_op jit(solution)/shard_map/reduce_scatter | solution.py:224
  451.9 6.4 %fusion.2 = bf16[512,2048]{1,0:T(8,128)(2,1)} fusion(bf16[352,2048]{1,0:T(8,128)(2,1)S(1)} %copy-done.14, bf16[1,512,2048]{2,1,0:T(8,128)(2,1)} %reduce-scatter.6.cloned.1.call-done, bf16[2048,352]{0,1:T(8,128)(2,1)} %param.36, bf16[8,512,2048]{2,1,0:T(8,128)(2,1)} %bitcast.107, s32[]{:T(128)S(6)} %select_n.105, f32[512,352]{0,1:T(8,128)} %fusion.14), kind=kOutput, calls=%fused_computation.12 | convolution fusion | flops 1480622080 | bytes 9895940 | tf_op jit(solution)/shard_map/dot_general | solution.py:220
  458.4 0.2 select_reduce_fusion.2
  458.6 0.1 fusion.50
  458.6 0.1 fusion.51
  458.7 2.2 copy.80
  460.9 0.1 copy.81
  461.1 1.4 gather_fusion.1
  462.5 0.7 copy.82
  463.2 3.2 gather_fusion
  466.4 1.4 select_bitcast_fusion
  467.9 0.9 select_select_fusion
  468.8 33.6 %reduce-scatter.8.cloned.1.call-done = bf16[128,2048]{1,0:T(8,128)(2,1)} async-done(((bf16[512,2048]{1,0:T(8,128)(2,1)}), bf16[128,2048]{1,0:T(8,128)(2,1)}) %reduce-scatter.8.cloned.1.call-update) | async-done | bytes 524304 | tf_op jit(solution)/shard_map/reduce_scatter | solution.py:226
  502.4 2.4 fusion.39
  (45 shorter events, 0.2 us)
Async XLA Ops:
  7.2 59.6 %copy-start = (bf16[2048,768]{1,0:T(8,128)(2,1)S(1)}, bf16[2048,768]{1,0:T(8,128)(2,1)}, u32[]{:S(2)}) copy-start(bf16[2048,768]{1,0:T(8,128)(2,1)} %param.24) | copy-start | bytes 9437188
  7.2 53.0 %all-gather.3.cloned.1.call-start = ((), (), s32[]{:S(2)}) async-start(), calls=%async_computation.3 | async-start | bytes 2621440 | tf_op jit(solution)/shard_map/all_gather | solution.py:116
  11.4 111.1 %reduce-scatter.4.cloned.1.call-start = ((), (), s32[]{:S(2)}) async-start(), calls=%async_computation.4 | async-start | bytes 2621440 | tf_op jit(solution)/shard_map/reduce_scatter | solution.py:181
  60.2 4.1 copy-start.5
  64.0 1.1 copy-start.6
  64.0 2.7 copy-start.12
  64.3 0.8 copy-start.4
  69.4 3.3 copy-start.7
  72.7 4.4 copy-start.11
  77.1 2.8 copy-start.10
  77.1 45.4 %copy-start.3 = (bf16[1,128,2048]{2,1,0:T(8,128)(2,1)S(1)}, bf16[1,128,2048]{2,1,0:T(8,128)(2,1)}, u32[]{:S(2)}) copy-start(bf16[1,128,2048]{2,1,0:T(8,128)(2,1)} %param.19) | copy-start | bytes 1572868
  77.2 48.8 %copy-start.9 = (s32[1,512,6]{1,0,2:T(1,128)S(1)}, s32[1,512,6]{1,0,2:T(1,128)}, u32[]{:S(2)}) copy-start(s32[1,512,6]{1,0,2:T(1,128)} %param.22) | copy-start | bytes 36868
  79.8 161.0 %all-gather.5.cloned.1.call-start = ((), (), s32[]{:S(2)}) async-start(), calls=%async_computation.5 | async-start | bytes 17301504 | tf_op jit(solution)/shard_map/all_gather | solution.py:187
  125.9 326.0 %reduce-scatter.6.cloned.1.call-start = ((), (), s32[]{:S(2)}) async-start(), calls=%async_computation.6 | async-start | bytes 18874368 | tf_op jit(solution)/shard_map/reduce_scatter | solution.py:224
  258.3 16.1 %copy-start.2 = (bf16[4096,2048]{1,0:T(8,128)(2,1)S(1)}, bf16[4096,2048]{1,0:T(8,128)(2,1)}, u32[]{:S(2)}) copy-start(bf16[4096,2048]{1,0:T(8,128)(2,1)} %all-gather.5.cloned.1.call-done) | copy-start | bytes 50331652
  258.3 16.1 %copy-start.8 = (bf16[2048,64]{0,1:T(8,128)(2,1)S(1)}, bf16[2048,64]{0,1:T(8,128)(2,1)}, u32[]{:S(2)}) copy-start(bf16[2048,64]{0,1:T(8,128)(2,1)} %param.31) | copy-start | bytes 786436
  337.6 1.4 copy-start.13
  337.6 114.3 %copy-start.14 = (bf16[352,2048]{1,0:T(8,128)(2,1)S(1)}, bf16[352,2048]{1,0:T(8,128)(2,1)}, u32[]{:S(2)}) copy-start(bf16[352,2048]{1,0:T(8,128)(2,1)} %param.37) | copy-start | bytes 4325380
  337.6 164.7 %reduce-scatter.8.cloned.1.call-start = ((), (), s32[]{:S(2)}) async-start(), calls=%async_computation.7 | async-start | bytes 2621440 | tf_op jit(solution)/shard_map/reduce_scatter | solution.py:226
  458.7 46.0 %copy-start.1 = (bf16[2048,768]{1,0:T(8,128)(2,1)S(1)}, bf16[2048,768]{1,0:T(8,128)(2,1)}, u32[]{:S(2)}) copy-start(bf16[2048,768]{1,0:T(8,128)(2,1)} %param.24) | copy-start | bytes 9437188
Sparse Core Ops, SparseCore 0:
  11.5 48.6 all-gather.2
  80.0 42.5 reduce-scatter.3
  126.6 114.2 all-gather.4
  337.7 114.1 reduce-scatter.5
  458.5 43.8 reduce-scatter.7
